TPU v7x, 32 devices: a whole 2x2x4 slice. The times are simulated.
32 devices in a mesh: prompts: 2 (over y), patch: 4 (over z), cfg: 2 (over core), batch: 2 (over x).
Axes of the slice: x: 2, y: 2, z: 4, core: 2. Of those that a mesh axis runs over, the one named last changes fastest.
Arguments:
- latent: float32 [4, 64, 1280], P(('prompts', 'batch'), 'patch'), parts along dimension 0, may hold values from -16 to 16
- stale_keys: bfloat16 [4, 64, 1280], P('prompts', 'patch', 'batch'), parts along dimension 0, may hold values from -18 to 18
- stale_values: bfloat16 [4, 64, 1280], P('prompts', 'patch', 'batch'), parts along dimension 0, may hold values from -12 to 12
- text_keys: bfloat16 [4, 77, 1280], P(('prompts', 'cfg'), None, 'batch'), parts along dimension 0, may hold values from -160 to 160
- text_values: bfloat16 [4, 77, 1280], P(('prompts', 'cfg'), None, 'batch'), parts along dimension 0, may hold values from -6 to 6
- w_query: bfloat16 [1280, 1280], P(None, 'batch'), may hold values from -0.15625 to 0.15625
- w_key: bfloat16 [1280, 1280], P(None, 'batch'), may hold values from -0.15625 to 0.15625
- w_value: bfloat16 [1280, 1280], P(None, 'batch'), may hold values from -0.15625 to 0.15625
- w_out: bfloat16 [1280, 1280], P('batch'), may hold values from -0.15625 to 0.15625
- norm_gain: float32 [1280], replicated, may hold values from 0.25 to 1.75
- norm_bias: float32 [1280], replicated, may hold values from -0.5 to 0.5
- timesteps: int32 [6], P('prompts'), parts along dimension 0, may hold values from 0 to 999, as said below
Outputs:
- final_latent: float32 [4, 64, 1280], P(('prompts', 'batch'), 'patch'), parts along dimension 0
- final_keys: bfloat16 [4, 64, 1280], P('prompts', 'patch', 'batch'), parts along dimension 0
- final_values: bfloat16 [4, 64, 1280], P('prompts', 'patch', 'batch'), parts along dimension 0
There are 2 independent parts, one for each index of `prompts`. A program takes and returns all parts, laid end to end along the dimension named above; an argument that names none is the same for every part. Nothing has to cross between parts.
Inputs may be any that keep to these rules, and one draw needn't show every extreme that they name: `timesteps`: strictly falling from the first entry to the last.
All inputs are finite; a program needn't handle non-finite values.
Results may differ from a plain program's by a relative error of at most 0.035.
Values may be sent and summed in bfloat16 or wider, within the bound.
A program may use at most 64 MiB of HBM per device.

v0:
```python
import math

import jax
import jax.numpy as jnp
from jax import lax
from jax.sharding import PartitionSpec as P

HEAD = 64
GROUPS = 32
STEPS = 2


guide_weight = 5.0
norm_eps = 1e-06


def from_partner(shard, axis, stride):
    return lax.ppermute(shard, axis, [(i, i ^ 1 << stride) for i in range(lax.axis_size(axis))])


def alpha_bar(step_index):
    grid = jnp.arange(1000, dtype=jnp.int32)
    ramp = grid.astype(jnp.float32) / 999.0
    root = math.sqrt(0.00085) + ramp * (math.sqrt(0.012) - math.sqrt(0.00085))
    logs = jnp.cumsum(jnp.log1p(-root * root))
    picked = (grid == step_index).astype(jnp.float32)
    return jnp.exp(jnp.sum(picked * logs))


def sampler_weights(now, after):
    a_now = alpha_bar(now)
    a_next = alpha_bar(after)
    keep = jnp.sqrt(a_next / a_now)
    push = jnp.sqrt(1.0 - a_next) - keep * jnp.sqrt(1.0 - a_now)
    return (keep, push)


def split_heads(block):
    return block.reshape(block.shape[0], block.shape[1], block.shape[2] // HEAD, HEAD)


def block_scores(queries, keys):
    return jnp.einsum(
        "bqhd,bkhd->bhqk", queries, keys, preferred_element_type=jnp.float32
    ) * HEAD ** (-0.5)


def body(
    latent,
    stale_keys,
    stale_values,
    text_keys,
    text_values,
    w_query,
    w_key,
    w_value,
    w_out,
    norm_gain,
    norm_bias,
    timesteps,
):
    state = latent[0]
    tok_rows = state.shape[0]
    width = state.shape[1]
    images = stale_keys.shape[0]
    local_width = w_query.shape[1]
    w_joint = jnp.concatenate([w_query, w_key, w_value], axis=1)
    patch_index = lax.axis_index("patch")
    half_index = lax.axis_index("cfg")
    group_width = width // GROUPS
    count = float(tok_rows * lax.axis_size("patch") * group_width)
    text_k = jnp.broadcast_to(text_keys, (images,) + text_keys.shape[1:])
    text_v = jnp.broadcast_to(text_values, (images,) + text_values.shape[1:])
    prior_k, prior_v = (stale_keys, stale_values)
    for step in range(STEPS):
        grouped = state.reshape(tok_rows, GROUPS, group_width)
        sums = jnp.sum(grouped, axis=(0, 2))
        squares = jnp.sum(grouped * grouped, axis=(0, 2))
        sums, squares = lax.psum((sums, squares), "patch")
        mean = sums / count
        scale = lax.rsqrt(squares / count - mean * mean + norm_eps)
        normed = ((grouped - mean[None, :, None]) * scale[None, :, None]).reshape(
            tok_rows, width
        ) * norm_gain + norm_bias
        normed = normed.astype(jnp.bfloat16)[None]
        piece = lax.all_gather(normed, "batch", axis=0, tiled=True)
        flat = piece.reshape(piece.shape[0] * tok_rows, width)
        joint_rows = jnp.dot(flat, w_joint, preferred_element_type=jnp.float32).astype(jnp.bfloat16)
        joint = joint_rows.reshape(piece.shape[0], tok_rows, 3 * local_width)
        queries = split_heads(joint[:, :, :local_width])
        fresh_k = joint[:, :, local_width : 2 * local_width]
        fresh_v = joint[:, :, 2 * local_width :]
        near_k = split_heads(jnp.concatenate([fresh_k, text_k], axis=1))
        near_v = split_heads(jnp.concatenate([fresh_v, text_v], axis=1))
        scores = block_scores(queries, near_k)
        top = jnp.max(scores, axis=-1)
        weights = jnp.exp(scores - top[..., None])
        start_acc = jnp.einsum(
            "bhqk,bkhd->bhqd",
            weights.astype(jnp.bfloat16),
            near_v,
            preferred_element_type=jnp.float32,
        )
        top_old = top
        total_old = jnp.sum(weights, axis=-1)
        piece_k = lax.all_gather(prior_k, "patch", axis=1, tiled=True)
        piece_v = lax.all_gather(prior_v, "patch", axis=1, tiled=True)
        piece_scores = block_scores(queries, split_heads(piece_k))
        place = jnp.arange(piece_k.shape[1], dtype=jnp.int32)
        own_rows = place // tok_rows == patch_index
        piece_scores = jnp.where(own_rows[None, None, None, :], -1e30, piece_scores)
        top_new = jnp.maximum(top_old, jnp.max(piece_scores, axis=-1))
        fade = jnp.exp(top_old - top_new)
        piece_weights = jnp.exp(piece_scores - top_new[..., None])
        total_new = total_old * fade + jnp.sum(piece_weights, axis=-1)
        acc_new = start_acc * fade[..., None] + jnp.einsum(
            "bhqk,bkhd->bhqd",
            piece_weights.astype(jnp.bfloat16),
            split_heads(piece_v),
            preferred_element_type=jnp.float32,
        )
        top = top_new
        attended = jnp.transpose(acc_new / total_new[..., None], (0, 2, 1, 3)).astype(jnp.bfloat16)
        attended = attended.reshape(images, tok_rows, local_width)
        rows_all = attended.reshape(images * tok_rows, local_width)
        mixed = lax.psum_scatter(
            jnp.dot(rows_all, w_out, preferred_element_type=jnp.float32).astype(jnp.bfloat16),
            "batch",
            scatter_dimension=0,
            tiled=True,
        ).astype(jnp.float32)
        branch = state + mixed
        other = from_partner(branch, "cfg", 0)
        leading = half_index == 0
        cond = jnp.where(leading, branch, other)
        uncond = jnp.where(leading, other, branch)
        guess = uncond + guide_weight * (cond - uncond)
        keep, push = sampler_weights(timesteps[step], timesteps[step + 1])
        state = keep * state + push * guess
        prior_k, prior_v = (fresh_k, fresh_v)
    return (state[None], prior_k, prior_v)


def solution(mesh):
    return jax.shard_map(
        body,
        mesh=mesh,
        in_specs=(
            P(("prompts", "batch"), "patch", None),
            P("prompts", "patch", "batch"),
            P("prompts", "patch", "batch"),
            P(("prompts", "cfg"), None, "batch"),
            P(("prompts", "cfg"), None, "batch"),
            P(None, "batch"),
            P(None, "batch"),
            P(None, "batch"),
            P("batch", None),
            P(),
            P(),
            P("prompts"),
        ),
        out_specs=(
            P(("prompts", "batch"), "patch", None),
            P("prompts", "patch", "batch"),
            P("prompts", "patch", "batch"),
        ),
        check_vma=False,
    )
```

profile of v0, /device:TPU:0, one launch (start us, length us, event | category | flops | bytes accessed | tf_op | source)
XLA Modules:
  0.0 152.7 jit_solution(90200097315867511)
XLA Ops:
  7.2 1.1 fusion.36
  8.7 13.5 %all-reduce.2 = (f32[32]{0:T(128)S(1)}, f32[32]{0:T(128)S(1)}) all-reduce(f32[32]{0:T(128)S(1)} %reduce_sum.147, f32[32]{0:T(128)S(1)} %reduce_sum.144), channel_id=1, replica_groups=mesh['prompts'=2,'patch'=4,'cfg'=2,'batch'=2] {'patch'}, use_global_device_ids=true, to_apply=%region_10.11 | all-reduce | flops 64 | bytes 512 | tf_op jit(solution)/shard_map/psum | solution.py:79
  22.5 1.1 add_convert_fusion.1
  23.6 4.7 %all_gather.18 = bf16[2,16,1280]{2,1,0:T(8,128)(2,1)S(1)} all-gather(bf16[1,16,1280]{2,1,0:T(8,128)(2,1)S(1)} %add_convert_fusion.1), channel_id=1, replica_groups=mesh['prompts'=2,'patch'=4,'cfg'=2,'batch'=2] {'batch'}, dimensions={0}, use_global_device_ids=true | all-gather | bytes 122880 | tf_op jit(solution)/shard_map/all_gather | solution.py:86
  28.3 1.6 %constant_dynamic-update-slice_fusion.2 = bf16[1280,1920]{1,0:T(8,128)(2,1)S(1)} fusion(bf16[1280,640]{1,0:T(8,128)(2,1)} %param.17), kind=kLoop, calls=%fused_computation.65 | loop fusion | bytes 3276800
  30.5 2.2 %copy-done.1 = bf16[1280,1920]{1,0:T(8,128)(2,1)} copy-done((bf16[1280,1920]{1,0:T(8,128)(2,1)}, bf16[1280,1920]{1,0:T(8,128)(2,1)S(1)}, u32[]{:S(2)}) %copy-start.1) | copy-done | bytes 4915224
  32.7 0.9 convolution_convert_fusion.3
  34.3 13.5 %all_gather.19 = bf16[2,64,640]{2,0,1:T(2,128)(2,1)S(1)} all-gather(bf16[2,16,640]{2,0,1:T(2,128)(2,1)S(1)} %copy.70), channel_id=1, replica_groups=mesh['prompts'=2,'patch'=4,'cfg'=2,'batch'=2] {'patch'}, dimensions={1}, use_global_device_ids=true | all-gather | bytes 204800 | tf_op jit(solution)/shard_map/all_gather | solution.py:106
  49.5 0.8 copy.74
  50.3 13.5 %all_gather.20 = bf16[2,64,640]{2,0,1:T(2,128)(2,1)S(1)} all-gather(bf16[2,16,640]{2,0,1:T(2,128)(2,1)S(1)} %copy.74), channel_id=1, replica_groups=mesh['prompts'=2,'patch'=4,'cfg'=2,'batch'=2] {'patch'}, dimensions={1}, use_global_device_ids=true | all-gather | bytes 204800 | tf_op jit(solution)/shard_map/all_gather | solution.py:107
  63.8 1.0 copy.75
  65.6 1.3 fusion.8
  67.1 1.0 convolution_convert_fusion.1
  68.7 0.6 fusion.42
  69.4 2.5 %select_reduce_fusion.2 = (f32[]{:T(128)}, f32[]{:T(128)}, f32[]{:T(128)}) fusion(f32[1024]{0:T(1024)S(1)} %add_bitcast_fusion.1, s32[]{:T(128)} %bitcast, s32[]{:T(128)} %bitcast.3, s32[]{:T(128)} %bitcast.4), kind=kLoop, calls=%fused_computation.73 | loop fusion | flops 8997 | bytes 4024 | tf_op jit(solution)/shard_map/reduce_sum | solution.py:27
  71.9 4.5 %reduce-scatter.3.cloned.1.call-done = bf16[16,1280]{1,0:T(8,128)(2,1)} async-done(((bf16[32,1280]{1,0:T(8,128)(2,1)}), bf16[16,1280]{1,0:T(8,128)(2,1)}) %reduce-scatter.3.cloned.1.call-update) | async-done | bytes 40976 | tf_op jit(solution)/shard_map/reduce_scatter | solution.py:126
  76.4 0.8 bitcast_add_fusion
  77.3 13.6 %all_gather.22 = bf16[2,64,640]{2,0,1:T(2,128)(2,1)S(1)} all-gather(bf16[2,16,640]{2,0,1:T(2,128)(2,1)S(1)} %copy.91), channel_id=1, replica_groups=mesh['prompts'=2,'patch'=4,'cfg'=2,'batch'=2] {'patch'}, dimensions={1}, use_global_device_ids=true | all-gather | bytes 204800 | tf_op jit(solution)/shard_map/all_gather | solution.py:106
  92.8 13.7 %all_gather.23 = bf16[2,64,640]{2,0,1:T(2,128)(2,1)S(1)} all-gather(bf16[2,16,640]{2,0,1:T(2,128)(2,1)S(1)} %copy.92), channel_id=1, replica_groups=mesh['prompts'=2,'patch'=4,'cfg'=2,'batch'=2] {'patch'}, dimensions={1}, use_global_device_ids=true | all-gather | bytes 204800 | tf_op jit(solution)/shard_map/all_gather | solution.py:107
  106.5 1.0 copy.84
  107.5 0.8 fusion.35
  108.7 11.7 %all-reduce.1 = (f32[32]{0:T(128)S(1)}, f32[32]{0:T(128)S(1)}) all-reduce(f32[32]{0:T(128)S(1)} %reduce_sum.157, f32[32]{0:T(128)S(1)} %reduce_sum.154), channel_id=1, replica_groups=mesh['prompts'=2,'patch'=4,'cfg'=2,'batch'=2] {'patch'}, use_global_device_ids=true, to_apply=%region_21.22 | all-reduce | flops 64 | bytes 512 | tf_op jit(solution)/shard_map/psum | solution.py:79
  120.9 4.7 %all-gather = bf16[32,1280]{1,0:T(8,128)(2,1)S(1)} all-gather(bf16[16,1280]{1,0:T(8,128)(2,1)S(1)} %add_convert_fusion), channel_id=2, replica_groups=mesh['prompts'=2,'patch'=4,'cfg'=2,'batch'=2] {'batch'}, dimensions={0}, use_global_device_ids=true | all-gather | bytes 122880 | tf_op jit(solution)/shard_map/all_gather | solution.py:86
  125.5 3.3 %convolution_convert_fusion.2 = bf16[32,1920]{1,0:T(8,128)(2,1)S(1)} fusion(bf16[32,1280]{1,0:T(8,128)(2,1)S(1)} %all-gather, bf16[1280,1920]{1,0:T(8,128)(2,1)} %copy-done.1), kind=kOutput, calls=%fused_computation.2 | convolution fusion | flops 157347840 | bytes 5120000 | tf_op jit(solution)/shard_map/dot_general | solution.py:88
  128.9 0.6 fusion.40
  129.5 0.6 copy-done.5
  131.5 1.0 copy.80
  133.3 1.3 fusion.9
  134.8 1.0 convolution_convert_fusion
  135.8 7.3 %reduce-scatter.5.cloned.1.call-done = bf16[16,1280]{1,0:T(8,128)(2,1)} async-done(((bf16[32,1280]{1,0:T(8,128)(2,1)}), bf16[16,1280]{1,0:T(8,128)(2,1)}) %reduce-scatter.5.cloned.1.call-update) | async-done | bytes 40976 | tf_op jit(solution)/shard_map/reduce_scatter | solution.py:126
  143.1 0.8 convert_add_fusion
  145.2 0.7 add_bitcast_fusion
  (96 shorter events, 9.2 us)
Async XLA Ops:
  7.2 59.9 %copy-start = (bf16[640,1280]{1,0:T(8,128)(2,1)S(1)}, bf16[640,1280]{1,0:T(8,128)(2,1)}, u32[]{:S(2)}) copy-start(bf16[640,1280]{1,0:T(8,128)(2,1)} %param.20) | copy-start | bytes 4915204
  7.2 22.7 %copy-start.2 = (bf16[1280,640]{1,0:T(8,128)(2,1)S(1)}, bf16[1280,640]{1,0:T(8,128)(2,1)}, u32[]{:S(2)}) copy-start(bf16[1280,640]{1,0:T(8,128)(2,1)} %param.18) | copy-start | bytes 4915204
  7.2 69.2 %reduce-scatter.3.cloned.1.call-start = ((), (), s32[]{:S(2)}) async-start(), calls=%async_computation.2 | async-start | bytes 122880 | tf_op jit(solution)/shard_map/reduce_scatter | solution.py:126
  22.5 7.6 %copy-start.3 = (bf16[1280,640]{1,0:T(8,128)(2,1)S(1)}, bf16[1280,640]{1,0:T(8,128)(2,1)}, u32[]{:S(2)}) copy-start(bf16[1280,640]{1,0:T(8,128)(2,1)} %param.19) | copy-start | bytes 4915204
  30.1 3.7 %copy-start.6 = (bf16[1,77,640]{2,1,0:T(8,128)(2,1)S(1)}, bf16[1,77,640]{2,1,0:T(8,128)(2,1)}, u32[]{:S(2)}) copy-start(bf16[1,77,640]{2,1,0:T(8,128)(2,1)} %param.15) | copy-start | bytes 295684
  30.2 4.0 %copy-start.8 = (bf16[2,16,640]{2,1,0:T(8,128)(2,1)S(1)}, bf16[2,16,640]{2,1,0:T(8,128)(2,1)}, u32[]{:S(2)}) copy-start(bf16[2,16,640]{2,1,0:T(8,128)(2,1)} %param.13) | copy-start | bytes 122884
  30.5 2.2 %copy-start.1 = (bf16[1280,1920]{1,0:T(8,128)(2,1)}, bf16[1280,1920]{1,0:T(8,128)(2,1)S(1)}, u32[]{:S(2)}) copy-start(bf16[1280,1920]{1,0:T(8,128)(2,1)S(1)} %constant_dynamic-update-slice_fusion) | copy-start | bytes 14745604
  32.7 16.7 %copy-start.7 = (bf16[1,77,640]{2,1,0:T(8,128)(2,1)S(1)}, bf16[1,77,640]{2,1,0:T(8,128)(2,1)}, u32[]{:S(2)}) copy-start(bf16[1,77,640]{2,1,0:T(8,128)(2,1)} %param.16) | copy-start | bytes 295684
  48.1 20.7 %copy-start.11 = (s32[3]{0:T(128)S(1)}, s32[3]{0:T(128)}, u32[]{:S(2)}) copy-start(s32[3]{0:T(128)} %param.23) | copy-start | bytes 40
  48.1 28.4 %copy-start.4 = (f32[1,16,1280]{2,1,0:T(8,128)S(1)}, f32[1,16,1280]{2,1,0:T(8,128)}, u32[]{:S(2)}) copy-start(f32[1,16,1280]{2,1,0:T(8,128)} %param.12) | copy-start | bytes 245764
  48.8 72.0 %copy-start.9 = (f32[1280]{0:T(1024)S(1)}, f32[1280]{0:T(1024)}, u32[]{:S(2)}) copy-start(f32[1280]{0:T(1024)} %param.22) | copy-start | bytes 15364
  48.9 72.0 %copy-start.10 = (f32[1280]{0:T(1024)S(1)}, f32[1280]{0:T(1024)}, u32[]{:S(2)}) copy-start(f32[1280]{0:T(1024)} %param.21) | copy-start | bytes 15364
  68.1 75.0 %reduce-scatter.5.cloned.1.call-start = ((), (), s32[]{:S(2)}) async-start(), calls=%async_computation.3 | async-start | bytes 122880 | tf_op jit(solution)/shard_map/reduce_scatter | solution.py:126
  77.2 30.3 %collective-permute-start = (f32[16,1280]{1,0:T(8,128)S(1)}, f32[16,1280]{1,0:T(8,128)S(1)}, u32[]{:S(2)}, u32[]{:S(2)}) collective-permute-start(f32[16,1280]{1,0:T(8,128)S(1)} %bitcast_add_fusion), channel_id=1, source_target_pairs={{0,2},{2,0},{1,3},{3,1},{4,6},{6,4},{5,7},{7,5},{8,10},{10,8},{9,1... | collective-permute-start | bytes 245768 | tf_op jit(solution)/shard_map/ppermute | solution.py:18
  129.5 0.6 copy-start.5
  143.9 1.3 collective-permute-start.1
Sparse Core Ops, SparseCore 0:
  68.2 8.1 reduce-scatter.2
  135.9 7.1 reduce-scatter.4
where the time goes:
time: 153 us
  blocking collectives  88.9 us (58%)
  between operations  16.9 us (11%)
  local copies, waits for them, and re-layouts  13.4 us (9%)
  waiting for transfers between devices  12.4 us (8%)
  matrix products  10.7 us (7%)
  other arithmetic  10.2 us (7%)
    all_gather x2, blocking collectives, body(): piece_v = lax.all_gather(prior_v, 'patch', axis=1, tiled=True)  27.2 us
    all_gather x2, blocking collectives, body(): piece_k = lax.all_gather(prior_k, 'patch', axis=1, tiled=True)  27.1 us
    psum x2, blocking collectives, body(): sums, squares = lax.psum((sums, squares), 'patch')  25.2 us
    reduce_scatter x2, waiting for transfers between devices, body(): lax.psum_scatter(jnp.dot(rows_all, w_out, preferred_element_type=jnp.floa...  11.9 us
    all_gather x2, blocking collectives, body(): piece = lax.all_gather(normed, 'batch', axis=0, tiled=True)  9.36 us
    unnamed x30, local copies, waits for them, and re-layouts  5.64 us
    dot_general x2, matrix products, body(): jnp.dot(flat, w_joint, preferred_element_type=jnp.float32)  4.26 us
  transfers between devices with their start and end apart: 4, of which 3 were waited for; matrix products, arithmetic and copies ran while one was open for 3% of the time, Pallas kernels for 0%

commit v1 on v0

v1 whole, which is shorter than its diff:
```python
import functools
import math

import jax
import jax.numpy as jnp
from jax import lax
from jax.experimental import pallas as pl
from jax.experimental.pallas import tpu as pltpu
from jax.sharding import PartitionSpec as P

HEAD = 64
GROUPS = 32
STEPS = 2
LANES = 128

guide_weight = 5.0
norm_eps = 1e-06
MESH = pl.DeviceIdType.MESH
F32 = jnp.float32
BF16 = jnp.bfloat16


def split3(x):
    hi = x.astype(BF16)
    rest = x - hi.astype(F32)
    mid = rest.astype(BF16)
    low = (rest - mid.astype(F32)).astype(BF16)
    return hi, mid, low


def exact_dot(x, onehot, contract):
    rows = x.shape[0]
    parts = jnp.concatenate([p.astype(F32) for p in split3(x)], axis=0).astype(BF16)
    out = lax.dot_general(parts, onehot, (((1,), (contract,)), ((), ())), preferred_element_type=F32)
    return out[:rows] + out[rows : 2 * rows] + out[2 * rows :]


def kernel(
    n_patch,
    n_batch,
    latent,
    stale_k,
    stale_v,
    text_k,
    text_v,
    w_query,
    w_key,
    w_value,
    w_out,
    gain,
    bias,
    timesteps,
    out_state,
    out_k,
    out_v,
    state_v,
    tk_v,
    tv_v,
    wq_v,
    wk_v,
    wv_v,
    wo_v,
    k_all,
    v_all,
    fresh_kv,
    dev_send,
    dev_recv,
    cen_send,
    cen_recv,
    stat_send,
    stat_all,
    mix_send,
    mix_all,
    load_sem,
    kv_send_sem,
    kv_recv_sem,
    dev_send_sem,
    dev_recv_sem,
    stat_send_sem,
    stat_recv_sem,
    mix_send_sem,
    mix_recv_sem,
):
    patch = lax.axis_index("patch")
    half = lax.axis_index("cfg")
    batch = lax.axis_index("batch")
    tok = state_v.shape[0]
    width = state_v.shape[1]
    images = k_all.shape[2]
    local = wq_v.shape[1]
    heads = local // HEAD
    group_width = width // GROUPS
    count = float(tok * n_patch * group_width)

    loads = [
        pltpu.make_async_copy(src, dst, load_sem.at[i])
        for i, (src, dst) in enumerate(
            [
                (latent.at[0], state_v),
                (w_key, wk_v),
                (w_value, wv_v),
                (w_query, wq_v),
                (text_k.at[0], tk_v),
                (text_v.at[0], tv_v),
                (w_out, wo_v),
            ]
        )
    ]
    for copy in loads:
        copy.start()

    def peer(p, c, b):
        return {"patch": p, "cfg": c, "batch": b}

    others_pb = [(dp, db) for db in range(n_batch) for dp in range(n_patch) if (dp, db) != (0, 0)]
    others_bc = [(db, dc) for db in range(n_batch) for dc in range(2) if (db, dc) != (0, 0)]

    def at_patch(d):
        return lax.rem(patch + d, n_patch) if d else patch

    def at_batch(d):
        return lax.rem(batch + d, n_batch) if d else batch

    def at_half(d):
        return lax.rem(half + d, 2) if d else half

    barrier = pltpu.get_barrier_semaphore()
    greeted = 0
    for dp, db in others_pb:
        pl.semaphore_signal(barrier, inc=1, device_id=peer(at_patch(dp), half, at_batch(db)), device_id_type=MESH)
        greeted += 1
    for db, dc in others_bc:
        if dc:
            pl.semaphore_signal(barrier, inc=1, device_id=peer(patch, at_half(dc), at_batch(db)), device_id_type=MESH)
            greeted += 1

    chan = lax.broadcasted_iota(jnp.int32, (width, LANES), 0)
    lane = lax.broadcasted_iota(jnp.int32, (width, LANES), 1)
    low = lane * group_width
    onehot = jnp.where((chan >= low) & (chan < low + group_width), 1.0, 0.0).astype(BF16)

    head_id = lax.broadcasted_iota(jnp.int32, (heads, tok, local), 0) * HEAD
    col_id = lax.broadcasted_iota(jnp.int32, (heads, tok, local), 2)
    head_mask = (col_id >= head_id) & (col_id < head_id + HEAD)

    sub = lax.broadcasted_iota(jnp.int32, (8, LANES), 0)
    lan = lax.broadcasted_iota(jnp.int32, (8, LANES), 1)
    grid = sub * LANES + lan
    ramp = grid.astype(F32) / 999.0
    root = math.sqrt(0.00085) + ramp * (math.sqrt(0.012) - math.sqrt(0.00085))
    logs = jnp.log1p(-root * root)

    def alpha_bar(t):
        picked = jnp.where((grid <= t) & (grid < 1000), logs, 0.0)
        return jnp.exp(jnp.sum(jnp.sum(picked, axis=1, keepdims=True), axis=0, keepdims=True))

    abar = [alpha_bar(timesteps[0, s]) for s in range(STEPS + 1)]

    def send_kv(step, src_k, src_v):
        made = []
        for d in range(1, n_patch):
            for j, (src, dst) in enumerate([(src_k, k_all), (src_v, v_all)]):
                copy = pltpu.make_async_remote_copy(
                    src_ref=src,
                    dst_ref=dst.at[step, :, :, pl.ds(pl.multiple_of(patch * tok, tok), tok), :].at[0],
                    send_sem=kv_send_sem.at[step, j, d],
                    recv_sem=kv_recv_sem.at[step, j, d],
                    device_id=peer(at_patch(d), half, batch),
                    device_id_type=MESH,
                )
                copy.start()
                made.append(copy)
        return made

    sent = []
    loads[0].wait()
    state = state_v[...]
    gain_row = gain[...]
    bias_row = bias[...]

    for step in range(STEPS):
        col_sum = jnp.sum(state, axis=0, keepdims=True)
        col_sq = jnp.sum(state * state, axis=0, keepdims=True)
        centre = col_sum / float(tok)
        cen_send[step] = centre
        dev_send[step] = (state - centre).astype(BF16)
        if step == 0:
            pl.semaphore_wait(barrier, greeted)
        dev_waits = []
        for d in range(1, n_batch):
            for j, (src, dst) in enumerate([(dev_send, dev_recv), (cen_send, cen_recv)]):
                copy = pltpu.make_async_remote_copy(
                    src_ref=src.at[step],
                    dst_ref=dst.at[step, d],
                    send_sem=dev_send_sem.at[step, j, d],
                    recv_sem=dev_recv_sem.at[step, j, d],
                    device_id=peer(patch, half, at_batch(d)),
                    device_id_type=MESH,
                )
                copy.start()
                dev_waits.append(copy)
        pad = jnp.zeros((6, width), F32)
        compact = exact_dot(jnp.concatenate([col_sum, col_sq, pad], axis=0), onehot, 0)
        stat_send[step] = compact
        stat_all[step, batch, patch] = compact
        stat_waits = []
        for dp, db in others_pb:
            copy = pltpu.make_async_remote_copy(
                src_ref=stat_send.at[step],
                dst_ref=stat_all.at[step, batch, patch],
                send_sem=stat_send_sem.at[step, db, dp],
                recv_sem=stat_recv_sem.at[step, db, dp],
                device_id=peer(at_patch(dp), half, at_batch(db)),
                device_id_type=MESH,
            )
            copy.start()
            stat_waits.append(copy)
        if step == 0:
            sent += send_kv(0, stale_k, stale_v)
            kv_waits = sent[-2 * (n_patch - 1) :]
        for copy in stat_waits:
            copy.wait()

        rows = []
        for d in range(n_batch):
            total = stat_all[step, at_batch(d), 0]
            for p in range(1, n_patch):
                total = total + stat_all[step, at_batch(d), p]
            total = total / count
            mean = total[0:1]
            scale = lax.rsqrt(total[1:2] - mean * mean + norm_eps)
            rows += [mean, scale]
        pad_rows = -len(rows) % 8
        if pad_rows:
            rows.append(jnp.zeros((pad_rows, LANES), F32))
        wide = exact_dot(jnp.concatenate(rows, axis=0), onehot, 1)
        for copy in dev_waits:
            copy.wait()
        pieces = []
        for d in range(n_batch):
            mean = wide[2 * d : 2 * d + 1]
            scale = wide[2 * d + 1 : 2 * d + 2]
            if d == 0:
                shifted = state - mean
            else:
                shifted = dev_recv[step, n_batch - d].astype(F32) + (cen_recv[step, n_batch - d] - mean)
            pieces.append((shifted * scale * gain_row + bias_row).astype(BF16))
        normed = jnp.concatenate(pieces, axis=0)

        own = pl.ds(pl.multiple_of(patch * tok, tok), tok)
        if step == 0:
            loads[1].wait()
        keys = jnp.dot(normed, wk_v[...], preferred_element_type=F32).astype(BF16)
        for d in range(n_batch):
            block = keys[d * tok : (d + 1) * tok]
            k_all[step, 0, at_batch(d), own, :] = block
            fresh_kv[step, 0, at_batch(d)] = block
        if step == 0:
            loads[2].wait()
        values = jnp.dot(normed, wv_v[...], preferred_element_type=F32).astype(BF16)
        for d in range(n_batch):
            block = values[d * tok : (d + 1) * tok]
            v_all[step, 0, at_batch(d), own, :] = block
            fresh_kv[step, 1, at_batch(d)] = block
        next_waits = []
        if step < STEPS - 1:
            next_waits = send_kv(step + 1, fresh_kv.at[step, 0], fresh_kv.at[step, 1])
        else:
            out_k[...] = fresh_kv[step, 0]
            out_v[...] = fresh_kv[step, 1]
        if step == 0:
            loads[3].wait()
        queries = jnp.dot(normed, wq_v[...], preferred_element_type=F32).astype(BF16)

        scaled = queries.astype(F32) * HEAD ** (-0.5)
        wide_q = []
        for d in range(n_batch):
            block = jnp.broadcast_to(scaled[d * tok : (d + 1) * tok][None], (heads, tok, local))
            wide_q.append(jnp.where(head_mask, block, 0.0).astype(BF16).reshape(heads * tok, local))
        if step == 0:
            loads[4].wait()
            loads[5].wait()
        nt = (((1,), (1,)), ((), ()))
        text_scores = lax.dot_general(
            jnp.concatenate(wide_q, axis=0), tk_v[...], nt, preferred_element_type=F32
        )
        for copy in kv_waits:
            copy.wait()
        kv_waits = next_waits
        attended = []
        span = heads * tok
        for d in range(n_batch):
            s_img = lax.dot_general(
                wide_q[d], k_all[step, 0, at_batch(d)], nt, preferred_element_type=F32
            )
            s_txt = text_scores[d * span : (d + 1) * span]
            top = jnp.maximum(
                jnp.max(s_img, axis=1, keepdims=True), jnp.max(s_txt, axis=1, keepdims=True)
            )
            e_img = jnp.exp(s_img - top)
            e_txt = jnp.exp(s_txt - top)
            inv = 1.0 / (jnp.sum(e_img, axis=1, keepdims=True) + jnp.sum(e_txt, axis=1, keepdims=True))
            full = jnp.dot(
                (e_img * inv).astype(BF16), v_all[step, 0, at_batch(d)], preferred_element_type=F32
            ) + jnp.dot((e_txt * inv).astype(BF16), tv_v[...], preferred_element_type=F32)
            full = jnp.where(head_mask, full.reshape(heads, tok, local), 0.0)
            attended.append(jnp.sum(full, axis=0))
        rows_all = jnp.concatenate(attended, axis=0).astype(BF16)

        if step == 0:
            loads[6].wait()
        partial = jnp.dot(rows_all, wo_v[...], preferred_element_type=F32).astype(BF16)
        for d in range(1, n_batch):
            mix_send[step, d] = partial[d * tok : (d + 1) * tok]
        mix_send[step, 0] = partial[:tok]
        mix_all[step, 2 * batch + half] = partial[:tok]
        mix_waits = []
        for db, dc in reversed(others_bc):
            copy = pltpu.make_async_remote_copy(
                src_ref=mix_send.at[step, db],
                dst_ref=mix_all.at[step, 2 * batch + half],
                send_sem=mix_send_sem.at[step, db, dc],
                recv_sem=mix_recv_sem.at[step, db, dc],
                device_id=peer(patch, at_half(dc), at_batch(db)),
                device_id_type=MESH,
            )
            copy.start()
            mix_waits.append(copy)
        for copy in mix_waits:
            copy.wait()
        cond = mix_all[step, 0].astype(F32)
        uncond = mix_all[step, 1].astype(F32)
        for b in range(1, n_batch):
            cond = cond + mix_all[step, 2 * b].astype(F32)
            uncond = uncond + mix_all[step, 2 * b + 1].astype(F32)
        guess = state + uncond + guide_weight * (cond - uncond)
        keep = jnp.sqrt(abar[step + 1] / abar[step])
        push = jnp.sqrt(1.0 - abar[step + 1]) - keep * jnp.sqrt(1.0 - abar[step])
        state = keep * state + push * guess
    out_state[0] = state


def body(
    n_patch, n_batch, latent, stale_keys, stale_values, text_keys, text_values,
    w_query, w_key, w_value, w_out, norm_gain, norm_bias, timesteps,
):
    _, tok, width = latent.shape
    images = stale_keys.shape[0]
    local = w_query.shape[1]
    ctx = text_keys.shape[1]
    any_spec = pl.BlockSpec(memory_space=pl.ANY)
    vmem = pl.BlockSpec(memory_space=pltpu.VMEM)
    dma = pltpu.SemaphoreType.DMA
    return pl.pallas_call(
        functools.partial(kernel, n_patch, n_batch),
        out_shape=(
            jax.ShapeDtypeStruct(latent.shape, F32),
            jax.ShapeDtypeStruct(stale_keys.shape, BF16),
            jax.ShapeDtypeStruct(stale_values.shape, BF16),
        ),
        in_specs=[any_spec] * 9 + [vmem] * 2 + [pl.BlockSpec(memory_space=pltpu.SMEM)],
        out_specs=(vmem, vmem, vmem),
        scratch_shapes=[
            pltpu.VMEM((tok, width), F32),
            pltpu.VMEM((ctx, local), BF16),
            pltpu.VMEM((ctx, local), BF16),
            pltpu.VMEM((width, local), BF16),
            pltpu.VMEM((width, local), BF16),
            pltpu.VMEM((width, local), BF16),
            pltpu.VMEM((local, width), BF16),
            pltpu.VMEM((STEPS, 1, images, n_patch * tok, local), BF16),
            pltpu.VMEM((STEPS, 1, images, n_patch * tok, local), BF16),
            pltpu.VMEM((STEPS, 2, images, tok, local), BF16),
            pltpu.VMEM((STEPS, tok, width), BF16),
            pltpu.VMEM((STEPS, n_batch, tok, width), BF16),
            pltpu.VMEM((STEPS, 1, width), F32),
            pltpu.VMEM((STEPS, n_batch, 1, width), F32),
            pltpu.VMEM((STEPS, 8, LANES), F32),
            pltpu.VMEM((STEPS, n_batch, n_patch, 8, LANES), F32),
            pltpu.VMEM((STEPS, n_batch, tok, width), BF16),
            pltpu.VMEM((STEPS, 2 * n_batch, tok, width), BF16),
            dma((7,)),
            dma((STEPS, 2, n_patch)),
            dma((STEPS, 2, n_patch)),
            dma((STEPS, 2, n_batch)),
            dma((STEPS, 2, n_batch)),
            dma((STEPS, n_batch, n_patch)),
            dma((STEPS, n_batch, n_patch)),
            dma((STEPS, n_batch, 2)),
            dma((STEPS, n_batch, 2)),
        ],
        compiler_params=pltpu.CompilerParams(
            collective_id=0, has_side_effects=True, vmem_limit_bytes=40 * 1024 * 1024
        ),
    )(
        latent, stale_keys, stale_values, text_keys, text_values, w_query, w_key, w_value, w_out,
        norm_gain.reshape(1, width), norm_bias.reshape(1, width), timesteps.reshape(1, -1),
    )


def solution(mesh):
    return jax.shard_map(
        functools.partial(body, mesh.shape["patch"], mesh.shape["batch"]),
        mesh=mesh,
        in_specs=(
            P(("prompts", "batch"), "patch", None),
            P("prompts", "patch", "batch"),
            P("prompts", "patch", "batch"),
            P(("prompts", "cfg"), None, "batch"),
            P(("prompts", "cfg"), None, "batch"),
            P(None, "batch"),
            P(None, "batch"),
            P(None, "batch"),
            P("batch", None),
            P(),
            P(),
            P("prompts"),
        ),
        out_specs=(
            P(("prompts", "batch"), "patch", None),
            P("prompts", "patch", "batch"),
            P("prompts", "patch", "batch"),
        ),
        check_vma=False,
    )
```

time: 153 us -> 52.9 us (0.35)
  blocking collectives: 88.9 us -> 0 us
  Pallas kernels: 0 us -> 37.8 us
  between operations: 16.9 us -> 0.65 us
  waiting for transfers between devices: 12.4 us -> 0 us
  matrix products: 10.7 us -> 0 us
  other arithmetic: 10.2 us -> 0 us
    all_gather x6 -> x0, blocking collectives: 63.7 us -> none  [the longest x2 27.2 us: body(): piece_v = lax.all_gather(prior_v, 'patch', axis=1, tiled=True)]
    pallas_call x0 -> x1, Pallas kernels: none -> 37.8 us  [body(): pl.pallas_call(functools.partial(kernel, n_patch, n_batch), out_shape=(ja...]
    psum x2 -> x0, blocking collectives: 25.2 us -> none  [body(): sums, squares = lax.psum((sums, squares), 'patch')]
    reduce_scatter x2 -> x0, waiting for transfers between devices: 11.9 us -> none  [body(): lax.psum_scatter(jnp.dot(rows_all, w_out, preferred_element_type=jnp.floa...]
    dot_general x12 -> x0, matrix products: 10.7 us -> none  [the longest x2 4.26 us: body(): jnp.dot(flat, w_joint, preferred_element_type=jnp.float32)]
    unnamed x30 -> x23, local copies, waits for them, and re-layouts: 5.64 us -> 12.5 us
    reduce_sum x11 -> x0, other arithmetic: 5.72 us -> none  [the longest x1 2.52 us: alpha_bar(): return jnp.exp(jnp.sum(picked * logs))]
    slice x8 -> x0, local copies, waits for them, and re-layouts: 2.97 us -> none  [the longest x2 1.22 us: body(): fresh_v = joint[:, :, 2 * local_width:]]
  transfers between devices with their start and end apart: 4 -> 0, of which waited for: 3 -> 0; matrix products, arithmetic and copies ran while one was open for 3% -> 0% of each run, Pallas kernels for 0% -> 0%
where the time goes in v1:
time: 52.9 us; the launch traced here: 52.3 us
  Pallas kernels  37.8 us (71%)
  local copies, waits for them, and re-layouts  13.9 us (26%)
  between operations  0.65 us (1%)
    pallas_call x1, Pallas kernels, body(): pl.pallas_call(functools.partial(kernel, n_patch, n_batch), out_shape=(ja...  37.8 us
    unnamed x23, local copies, waits for them, and re-layouts  12.5 us

profile of v1, /device:TPU:0, one launch (start us, length us, event | category | flops | bytes accessed | tf_op | source)
XLA Modules:
  0.0 52.3 jit_solution(14316110110287329172)
XLA Ops:
  0.6 0.7 %reshape.15.gain = f32[1,1280]{1,0:T(1,128)S(1)} reshape(f32[1280]{0:T(1024)} %param.21) | data formatting | bytes 10240 | tf_op jit(solution)/shard_map/reshape | solution.py:397
  1.3 0.7 %reshape.16.bias = f32[1,1280]{1,0:T(1,128)S(1)} reshape(f32[1280]{0:T(1024)} %param.22) | data formatting | bytes 10240 | tf_op jit(solution)/shard_map/reshape | solution.py:397
  2.0 0.0 copy-start
  2.0 1.4 %copy-done = bf16[1280,640]{1,0:T(8,128)(2,1)S(1)} copy-done((bf16[1280,640]{1,0:T(8,128)(2,1)S(1)}, bf16[1280,640]{1,0:T(8,128)(2,1)}, u32[]{:S(2)}) %copy-start) | copy-done | bytes 1638424
  3.5 0.0 copy-start.1
  3.5 1.4 %copy-done.1 = bf16[1280,640]{1,0:T(8,128)(2,1)S(1)} copy-done((bf16[1280,640]{1,0:T(8,128)(2,1)S(1)}, bf16[1280,640]{1,0:T(8,128)(2,1)}, u32[]{:S(2)}) %copy-start.1) | copy-done | bytes 1638424
  4.9 0.0 copy-start.2
  4.9 1.4 %copy-done.2 = bf16[1280,640]{1,0:T(8,128)(2,1)S(1)} copy-done((bf16[1280,640]{1,0:T(8,128)(2,1)S(1)}, bf16[1280,640]{1,0:T(8,128)(2,1)}, u32[]{:S(2)}) %copy-start.2) | copy-done | bytes 1638424
  6.3 0.0 copy-start.3
  6.3 1.4 %copy-done.3 = bf16[640,1280]{1,0:T(8,128)(2,1)S(1)} copy-done((bf16[640,1280]{1,0:T(8,128)(2,1)S(1)}, bf16[640,1280]{1,0:T(8,128)(2,1)}, u32[]{:S(2)}) %copy-start.3) | copy-done | bytes 1638424
  7.8 0.0 copy-start.4
  7.8 0.9 %copy-done.4 = bf16[1,77,640]{2,1,0:T(8,128)(2,1)S(1)} copy-done((bf16[1,77,640]{2,1,0:T(8,128)(2,1)S(1)}, bf16[1,77,640]{2,1,0:T(8,128)(2,1)}, u32[]{:S(2)}) %copy-start.4) | copy-done | bytes 98584
  8.7 0.0 copy-start.5
  8.7 0.9 %copy-done.5 = bf16[1,77,640]{2,1,0:T(8,128)(2,1)S(1)} copy-done((bf16[1,77,640]{2,1,0:T(8,128)(2,1)S(1)}, bf16[1,77,640]{2,1,0:T(8,128)(2,1)}, u32[]{:S(2)}) %copy-start.5) | copy-done | bytes 98584
  9.5 0.0 copy-start.6
  9.5 0.9 %copy-done.6 = f32[1,16,1280]{2,1,0:T(8,128)S(1)} copy-done((f32[1,16,1280]{2,1,0:T(8,128)S(1)}, f32[1,16,1280]{2,1,0:T(8,128)}, u32[]{:S(2)}) %copy-start.6) | copy-done | bytes 81944
  10.4 0.0 copy-start.7
  10.4 0.8 %copy-done.7 = bf16[2,16,640]{2,1,0:T(8,128)(2,1)S(1)} copy-done((bf16[2,16,640]{2,1,0:T(8,128)(2,1)S(1)}, bf16[2,16,640]{2,1,0:T(8,128)(2,1)}, u32[]{:S(2)}) %copy-start.7) | copy-done | bytes 40984
  11.2 0.0 copy-start.8
  11.2 0.8 %copy-done.8 = bf16[2,16,640]{2,1,0:T(8,128)(2,1)S(1)} copy-done((bf16[2,16,640]{2,1,0:T(8,128)(2,1)S(1)}, bf16[2,16,640]{2,1,0:T(8,128)(2,1)}, u32[]{:S(2)}) %copy-start.8) | copy-done | bytes 40984
  12.0 0.0 copy-start.9
  12.0 0.7 %copy-done.9 = s32[3]{0:T(128)S(1)} copy-done((s32[3]{0:T(128)S(1)}, s32[3]{0:T(128)}, u32[]{:S(2)}) %copy-start.9) | copy-done | bytes 36
  12.6 37.8 %shard_map.139 = (f32[1,16,1280]{2,1,0:T(8,128)S(1)}, bf16[2,16,640]{2,1,0:T(8,128)(2,1)S(1)}, bf16[2,16,640]{2,1,0:T(8,128)(2,1)S(1)}) custom-call(f32[1,16,1280]{2,1,0:T(8,128)S(1)} %copy-done.6, bf16[2,16,640]{2,1,0:T(8,128)(2,1)S(1)} %copy-done.7, bf16[2,16,640]{2,1,0:T(8,128)(2,1)S(1)} %copy-done.8, bf16[1,77,640]{2,1,0:T(8,128)(2,1)S(1)} %copy-done.4, ...), custom_call_target="tpu_custom_call" | custom-call | tf_op jit(solution)/shard_map/pallas_call | solution.py:354
  50.4 0.6 %copy.18 = f32[1,16,1280]{2,1,0:T(8,128)} copy(f32[1,16,1280]{2,1,0:T(8,128)S(1)} %get-tuple-element.6) | data formatting | bytes 163840
  51.1 0.6 %copy.19 = bf16[2,16,640]{2,1,0:T(8,128)(2,1)} copy(bf16[2,16,640]{2,1,0:T(8,128)(2,1)S(1)} %get-tuple-element.7) | data formatting | bytes 81920
  51.7 0.6 %copy.20 = bf16[2,16,640]{2,1,0:T(8,128)(2,1)} copy(bf16[2,16,640]{2,1,0:T(8,128)(2,1)S(1)} %get-tuple-element.8) | data formatting | bytes 81920
Async XLA Ops:
  2.0 1.4 %copy-start = (bf16[1280,640]{1,0:T(8,128)(2,1)S(1)}, bf16[1280,640]{1,0:T(8,128)(2,1)}, u32[]{:S(2)}) copy-start(bf16[1280,640]{1,0:T(8,128)(2,1)} %w_query.1) | copy-start | bytes 4915204
  3.5 1.4 %copy-start.1 = (bf16[1280,640]{1,0:T(8,128)(2,1)S(1)}, bf16[1280,640]{1,0:T(8,128)(2,1)}, u32[]{:S(2)}) copy-start(bf16[1280,640]{1,0:T(8,128)(2,1)} %w_key.1) | copy-start | bytes 4915204
  4.9 1.4 %copy-start.2 = (bf16[1280,640]{1,0:T(8,128)(2,1)S(1)}, bf16[1280,640]{1,0:T(8,128)(2,1)}, u32[]{:S(2)}) copy-start(bf16[1280,640]{1,0:T(8,128)(2,1)} %w_value.1) | copy-start | bytes 4915204
  6.3 1.4 %copy-start.3 = (bf16[640,1280]{1,0:T(8,128)(2,1)S(1)}, bf16[640,1280]{1,0:T(8,128)(2,1)}, u32[]{:S(2)}) copy-start(bf16[640,1280]{1,0:T(8,128)(2,1)} %w_out.1) | copy-start | bytes 4915204
  7.8 0.9 %copy-start.4 = (bf16[1,77,640]{2,1,0:T(8,128)(2,1)S(1)}, bf16[1,77,640]{2,1,0:T(8,128)(2,1)}, u32[]{:S(2)}) copy-start(bf16[1,77,640]{2,1,0:T(8,128)(2,1)} %text_k.1) | copy-start | bytes 295684
  8.7 0.9 %copy-start.5 = (bf16[1,77,640]{2,1,0:T(8,128)(2,1)S(1)}, bf16[1,77,640]{2,1,0:T(8,128)(2,1)}, u32[]{:S(2)}) copy-start(bf16[1,77,640]{2,1,0:T(8,128)(2,1)} %text_v.1) | copy-start | bytes 295684
  9.5 0.9 %copy-start.6 = (f32[1,16,1280]{2,1,0:T(8,128)S(1)}, f32[1,16,1280]{2,1,0:T(8,128)}, u32[]{:S(2)}) copy-start(f32[1,16,1280]{2,1,0:T(8,128)} %latent.1) | copy-start | bytes 245764
  10.4 0.8 %copy-start.7 = (bf16[2,16,640]{2,1,0:T(8,128)(2,1)S(1)}, bf16[2,16,640]{2,1,0:T(8,128)(2,1)}, u32[]{:S(2)}) copy-start(bf16[2,16,640]{2,1,0:T(8,128)(2,1)} %stale_k.1) | copy-start | bytes 122884
  11.2 0.8 %copy-start.8 = (bf16[2,16,640]{2,1,0:T(8,128)(2,1)S(1)}, bf16[2,16,640]{2,1,0:T(8,128)(2,1)}, u32[]{:S(2)}) copy-start(bf16[2,16,640]{2,1,0:T(8,128)(2,1)} %stale_v.1) | copy-start | bytes 122884
  12.0 0.7 %copy-start.9 = (s32[3]{0:T(128)S(1)}, s32[3]{0:T(128)}, u32[]{:S(2)}) copy-start(s32[3]{0:T(128)} %param.23) | copy-start | bytes 40

commit v2 on v1

--- a/solution.py
+++ b/solution.py
@@ -60,8 +60,8 @@
     wk_v,
     wv_v,
     wo_v,
-    k_all,
-    v_all,
+    kv_all,
+    stale_kv,
     fresh_kv,
     dev_send,
     dev_recv,
@@ -74,6 +74,8 @@
     load_sem,
     kv_send_sem,
     kv_recv_sem,
+    hand_send_sem,
+    hand_recv_sem,
     dev_send_sem,
     dev_recv_sem,
     stat_send_sem,
@@ -86,7 +88,7 @@
     batch = lax.axis_index("batch")
     tok = state_v.shape[0]
     width = state_v.shape[1]
-    images = k_all.shape[2]
+    images = kv_all.shape[2]
     local = wq_v.shape[1]
     heads = local // HEAD
     group_width = width // GROUPS
@@ -97,6 +99,8 @@
         for i, (src, dst) in enumerate(
             [
                 (latent.at[0], state_v),
+                (stale_k, stale_kv.at[0]),
+                (stale_v, stale_kv.at[1]),
                 (w_key, wk_v),
                 (w_value, wv_v),
                 (w_query, wq_v),
@@ -154,29 +158,47 @@
         picked = jnp.where((grid <= t) & (grid < 1000), logs, 0.0)
         return jnp.exp(jnp.sum(jnp.sum(picked, axis=1, keepdims=True), axis=0, keepdims=True))
 
-    abar = [alpha_bar(timesteps[0, s]) for s in range(STEPS + 1)]
-
-    def send_kv(step, src_k, src_v):
+    abar = [alpha_bar(timesteps[s]) for s in range(STEPS + 1)]
+
+    def slot(step, which, p):
+        return kv_all.at[step, which, :, pl.ds(pl.multiple_of(p * tok, tok), tok), :]
+
+    def send_kv(step, src):
         made = []
         for d in range(1, n_patch):
-            for j, (src, dst) in enumerate([(src_k, k_all), (src_v, v_all)]):
-                copy = pltpu.make_async_remote_copy(
-                    src_ref=src,
-                    dst_ref=dst.at[step, :, :, pl.ds(pl.multiple_of(patch * tok, tok), tok), :].at[0],
-                    send_sem=kv_send_sem.at[step, j, d],
-                    recv_sem=kv_recv_sem.at[step, j, d],
-                    device_id=peer(at_patch(d), half, batch),
-                    device_id_type=MESH,
-                )
-                copy.start()
-                made.append(copy)
+            copy = pltpu.make_async_remote_copy(
+                src_ref=src.at[half],
+                dst_ref=slot(step, half, patch),
+                send_sem=kv_send_sem.at[step, d],
+                recv_sem=kv_recv_sem.at[step, d],
+                device_id=peer(at_patch(d), half, batch),
+                device_id_type=MESH,
+            )
+            copy.start()
+            made.append(copy)
         return made
 
-    sent = []
+    def hand_over(step, arriving):
+        made = []
+        for d, copy in enumerate(arriving, 1):
+            copy.wait()
+            here = slot(step, half, at_patch(n_patch - d))
+            copy = pltpu.make_async_remote_copy(
+                src_ref=here,
+                dst_ref=here,
+                send_sem=hand_send_sem.at[step, d],
+                recv_sem=hand_recv_sem.at[step, d],
+                device_id=peer(patch, at_half(1), batch),
+                device_id_type=MESH,
+            )
+            copy.start()
+            made.append(copy)
+        return made
+
     loads[0].wait()
     state = state_v[...]
-    gain_row = gain[...]
-    bias_row = bias[...]
+    gain_row = gain[...].reshape(1, width)
+    bias_row = bias[...].reshape(1, width)
 
     for step in range(STEPS):
         col_sum = jnp.sum(state, axis=0, keepdims=True)
@@ -216,8 +238,11 @@
             copy.start()
             stat_waits.append(copy)
         if step == 0:
-            sent += send_kv(0, stale_k, stale_v)
-            kv_waits = sent[-2 * (n_patch - 1) :]
+            loads[1].wait()
+            loads[2].wait()
+            arriving = send_kv(0, stale_kv)
+        else:
+            handed = hand_over(step, arriving)
         for copy in stat_waits:
             copy.wait()
 
@@ -249,27 +274,24 @@
 
         own = pl.ds(pl.multiple_of(patch * tok, tok), tok)
         if step == 0:
-            loads[1].wait()
+            loads[3].wait()
         keys = jnp.dot(normed, wk_v[...], preferred_element_type=F32).astype(BF16)
         for d in range(n_batch):
             block = keys[d * tok : (d + 1) * tok]
-            k_all[step, 0, at_batch(d), own, :] = block
+            kv_all[step, 0, at_batch(d), own, :] = block
             fresh_kv[step, 0, at_batch(d)] = block
         if step == 0:
-            loads[2].wait()
+            loads[4].wait()
         values = jnp.dot(normed, wv_v[...], preferred_element_type=F32).astype(BF16)
         for d in range(n_batch):
             block = values[d * tok : (d + 1) * tok]
-            v_all[step, 0, at_batch(d), own, :] = block
+            kv_all[step, 1, at_batch(d), own, :] = block
             fresh_kv[step, 1, at_batch(d)] = block
-        next_waits = []
-        if step < STEPS - 1:
-            next_waits = send_kv(step + 1, fresh_kv.at[step, 0], fresh_kv.at[step, 1])
-        else:
+        if step == STEPS - 1:
             out_k[...] = fresh_kv[step, 0]
             out_v[...] = fresh_kv[step, 1]
         if step == 0:
-            loads[3].wait()
+            loads[5].wait()
         queries = jnp.dot(normed, wq_v[...], preferred_element_type=F32).astype(BF16)
 
         scaled = queries.astype(F32) * HEAD ** (-0.5)
@@ -278,20 +300,23 @@
             block = jnp.broadcast_to(scaled[d * tok : (d + 1) * tok][None], (heads, tok, local))
             wide_q.append(jnp.where(head_mask, block, 0.0).astype(BF16).reshape(heads * tok, local))
         if step == 0:
-            loads[4].wait()
-            loads[5].wait()
+            loads[6].wait()
+            loads[7].wait()
         nt = (((1,), (1,)), ((), ()))
         text_scores = lax.dot_general(
             jnp.concatenate(wide_q, axis=0), tk_v[...], nt, preferred_element_type=F32
         )
-        for copy in kv_waits:
+        if step == 0:
+            handed = hand_over(step, arriving)
+        if step < STEPS - 1:
+            arriving = send_kv(step + 1, fresh_kv.at[step])
+        for copy in handed:
             copy.wait()
-        kv_waits = next_waits
         attended = []
         span = heads * tok
         for d in range(n_batch):
             s_img = lax.dot_general(
-                wide_q[d], k_all[step, 0, at_batch(d)], nt, preferred_element_type=F32
+                wide_q[d], kv_all[step, 0, at_batch(d)], nt, preferred_element_type=F32
             )
             s_txt = text_scores[d * span : (d + 1) * span]
             top = jnp.maximum(
@@ -301,14 +326,14 @@
             e_txt = jnp.exp(s_txt - top)
             inv = 1.0 / (jnp.sum(e_img, axis=1, keepdims=True) + jnp.sum(e_txt, axis=1, keepdims=True))
             full = jnp.dot(
-                (e_img * inv).astype(BF16), v_all[step, 0, at_batch(d)], preferred_element_type=F32
+                (e_img * inv).astype(BF16), kv_all[step, 1, at_batch(d)], preferred_element_type=F32
             ) + jnp.dot((e_txt * inv).astype(BF16), tv_v[...], preferred_element_type=F32)
             full = jnp.where(head_mask, full.reshape(heads, tok, local), 0.0)
             attended.append(jnp.sum(full, axis=0))
         rows_all = jnp.concatenate(attended, axis=0).astype(BF16)
 
         if step == 0:
-            loads[6].wait()
+            loads[8].wait()
         partial = jnp.dot(rows_all, wo_v[...], preferred_element_type=F32).astype(BF16)
         for d in range(1, n_batch):
             mix_send[step, d] = partial[d * tok : (d + 1) * tok]
@@ -368,8 +393,8 @@
             pltpu.VMEM((width, local), BF16),
             pltpu.VMEM((width, local), BF16),
             pltpu.VMEM((local, width), BF16),
-            pltpu.VMEM((STEPS, 1, images, n_patch * tok, local), BF16),
-            pltpu.VMEM((STEPS, 1, images, n_patch * tok, local), BF16),
+            pltpu.VMEM((STEPS, 2, images, n_patch * tok, local), BF16),
+            pltpu.VMEM((2, images, tok, local), BF16),
             pltpu.VMEM((STEPS, 2, images, tok, local), BF16),
             pltpu.VMEM((STEPS, tok, width), BF16),
             pltpu.VMEM((STEPS, n_batch, tok, width), BF16),
@@ -379,9 +404,11 @@
             pltpu.VMEM((STEPS, n_batch, n_patch, 8, LANES), F32),
             pltpu.VMEM((STEPS, n_batch, tok, width), BF16),
             pltpu.VMEM((STEPS, 2 * n_batch, tok, width), BF16),
-            dma((7,)),
-            dma((STEPS, 2, n_patch)),
-            dma((STEPS, 2, n_patch)),
+            dma((9,)),
+            dma((STEPS, n_patch)),
+            dma((STEPS, n_patch)),
+            dma((STEPS, n_patch)),
+            dma((STEPS, n_patch)),
             dma((STEPS, 2, n_batch)),
             dma((STEPS, 2, n_batch)),
             dma((STEPS, n_batch, n_patch)),
@@ -390,11 +417,11 @@
             dma((STEPS, n_batch, 2)),
         ],
         compiler_params=pltpu.CompilerParams(
-            collective_id=0, has_side_effects=True, vmem_limit_bytes=40 * 1024 * 1024
+            collective_id=0, has_side_effects=True, vmem_limit_bytes=63 * 1024 * 1024
         ),
     )(
         latent, stale_keys, stale_values, text_keys, text_values, w_query, w_key, w_value, w_out,
-        norm_gain.reshape(1, width), norm_bias.reshape(1, width), timesteps.reshape(1, -1),
+        norm_gain, norm_bias, timesteps,
     )
 
 

time: 52.9 us -> 37.1 us (0.70)
  local copies, waits for them, and re-layouts: 13.9 us -> 4.32 us
  Pallas kernels: 37.8 us -> 31.8 us
    unnamed x23 -> x3, local copies, waits for them, and re-layouts: 12.5 us -> 4.32 us
    pallas_call x1, Pallas kernels: 37.8 us -> 31.8 us  [body(): pl.pallas_call(functools.partial(kernel, n_patch, n_batch), out_shape=(ja...]
    reshape x2 -> x0, local copies, waits for them, and re-layouts: 1.4 us -> none  [the longest x1 0.7 us: body(): norm_gain.reshape(1, width)]
where the time goes in v2:
time: 37.1 us; the launch traced here: 36.8 us
  Pallas kernels  31.8 us (86%)
  local copies, waits for them, and re-layouts  4.32 us (12%)
  between operations  0.64 us (2%)
    pallas_call x1, Pallas kernels, body(): pl.pallas_call(functools.partial(kernel, n_patch, n_batch), out_shape=(ja...  31.8 us
    unnamed x3, local copies, waits for them, and re-layouts  4.32 us

profile of v2, /device:TPU:0, one launch (start us, length us, event | category | flops | bytes accessed | tf_op | source)
XLA Modules:
  0.0 36.8 jit_solution(14956343417652271343)
XLA Ops:
  0.6 31.8 %shard_map.139 = (f32[1,16,1280]{2,1,0:T(8,128)}, bf16[2,16,640]{2,1,0:T(8,128)(2,1)}, bf16[2,16,640]{2,1,0:T(8,128)(2,1)}) custom-call(f32[1,16,1280]{2,1,0:T(8,128)} %latent.1, bf16[2,16,640]{2,1,0:T(8,128)(2,1)} %stale_k.1, bf16[2,16,640]{2,1,0:T(8,128)(2,1)} %stale_v.1, bf16[1,77,640]{2,1,0:T(8,128)(2,1)} %text_k.1, bf16[1,77,640]{2,1,0:T(8,128)(2,1)} %text_v.1, ...), custom_call_target="tpu_custom_call" | custom-call | tf_op jit(solution)/shard_map/pallas_call | solution.py:379
  32.4 1.5 %copy.18 = f32[1,16,1280]{2,1,0:T(8,128)} copy(f32[1,16,1280]{2,1,0:T(8,128)} %get-tuple-element.6) | data formatting | bytes 163840
  34.0 1.4 %copy.19 = bf16[2,16,640]{2,1,0:T(8,128)(2,1)} copy(bf16[2,16,640]{2,1,0:T(8,128)(2,1)} %get-tuple-element.7) | data formatting | bytes 81920
  35.4 1.4 %copy.20 = bf16[2,16,640]{2,1,0:T(8,128)(2,1)} copy(bf16[2,16,640]{2,1,0:T(8,128)(2,1)} %get-tuple-element.8) | data formatting | bytes 81920

commit v3 on v2

--- a/solution.py
+++ b/solution.py
@@ -54,6 +54,8 @@
     out_k,
     out_v,
     state_v,
+    gain_v,
+    bias_v,
     tk_v,
     tv_v,
     wq_v,
@@ -107,6 +109,8 @@
                 (text_k.at[0], tk_v),
                 (text_v.at[0], tv_v),
                 (w_out, wo_v),
+                (gain, gain_v),
+                (bias, bias_v),
             ]
         )
     ]
@@ -197,8 +201,6 @@
 
     loads[0].wait()
     state = state_v[...]
-    gain_row = gain[...].reshape(1, width)
-    bias_row = bias[...].reshape(1, width)
 
     for step in range(STEPS):
         col_sum = jnp.sum(state, axis=0, keepdims=True)
@@ -261,6 +263,11 @@
         wide = exact_dot(jnp.concatenate(rows, axis=0), onehot, 1)
         for copy in dev_waits:
             copy.wait()
+        if step == 0:
+            loads[9].wait()
+            loads[10].wait()
+            gain_row = gain_v[...].reshape(1, width)
+            bias_row = bias_v[...].reshape(1, width)
         pieces = []
         for d in range(n_batch):
             mean = wide[2 * d : 2 * d + 1]
@@ -373,20 +380,22 @@
     images = stale_keys.shape[0]
     local = w_query.shape[1]
     ctx = text_keys.shape[1]
-    any_spec = pl.BlockSpec(memory_space=pl.ANY)
+    hbm = pl.BlockSpec(memory_space=pl.ANY)
     vmem = pl.BlockSpec(memory_space=pltpu.VMEM)
     dma = pltpu.SemaphoreType.DMA
     return pl.pallas_call(
         functools.partial(kernel, n_patch, n_batch),
         out_shape=(
-            jax.ShapeDtypeStruct(latent.shape, F32),
-            jax.ShapeDtypeStruct(stale_keys.shape, BF16),
-            jax.ShapeDtypeStruct(stale_values.shape, BF16),
+            pltpu.VMEM(latent.shape, F32),
+            pltpu.VMEM(stale_keys.shape, BF16),
+            pltpu.VMEM(stale_values.shape, BF16),
         ),
-        in_specs=[any_spec] * 9 + [vmem] * 2 + [pl.BlockSpec(memory_space=pltpu.SMEM)],
+        in_specs=[hbm] * 11 + [pl.BlockSpec(memory_space=pltpu.SMEM)],
         out_specs=(vmem, vmem, vmem),
         scratch_shapes=[
             pltpu.VMEM((tok, width), F32),
+            pltpu.VMEM((width,), F32),
+            pltpu.VMEM((width,), F32),
             pltpu.VMEM((ctx, local), BF16),
             pltpu.VMEM((ctx, local), BF16),
             pltpu.VMEM((width, local), BF16),
@@ -404,7 +413,7 @@
             pltpu.VMEM((STEPS, n_batch, n_patch, 8, LANES), F32),
             pltpu.VMEM((STEPS, n_batch, tok, width), BF16),
             pltpu.VMEM((STEPS, 2 * n_batch, tok, width), BF16),
-            dma((9,)),
+            dma((11,)),
             dma((STEPS, n_patch)),
             dma((STEPS, n_patch)),
             dma((STEPS, n_patch)),
@@ -417,7 +426,7 @@
             dma((STEPS, n_batch, 2)),
         ],
         compiler_params=pltpu.CompilerParams(
-            collective_id=0, has_side_effects=True, vmem_limit_bytes=63 * 1024 * 1024
+            collective_id=0, has_side_effects=True, vmem_limit_bytes=62 * 1024 * 1024
         ),
     )(
         latent, stale_keys, stale_values, text_keys, text_values, w_query, w_key, w_value, w_out,

time: 37.1 us -> 33.7 us (0.908)
  local copies, waits for them, and re-layouts: 4.32 us -> 1.87 us
  Pallas kernels: 31.8 us -> 31.1 us
    unnamed x3, local copies, waits for them, and re-layouts: 4.32 us -> 1.87 us
    pallas_call x1, Pallas kernels: 31.8 us -> 31.1 us  [body(): pl.pallas_call(functools.partial(kernel, n_patch, n_batch), out_shape=(pl...]
where the time goes in v3:
time: 33.7 us; the launch traced here: 33.6 us
  Pallas kernels  31.1 us (92%)
  local copies, waits for them, and re-layouts  1.87 us (6%)
  between operations  0.64 us (2%)
    pallas_call x1, Pallas kernels, body(): pl.pallas_call(functools.partial(kernel, n_patch, n_batch), out_shape=(pl...  31.1 us
    unnamed x3, local copies, waits for them, and re-layouts  1.87 us

profile of v3, /device:TPU:0, one launch (start us, length us, event | category | flops | bytes accessed | tf_op | source)
XLA Modules:
  0.0 33.6 jit_solution(16065665237767667868)
XLA Ops:
  0.6 31.1 %shard_map.139 = (f32[1,16,1280]{2,1,0:T(8,128)S(1)}, bf16[2,16,640]{2,1,0:T(8,128)(2,1)S(1)}, bf16[2,16,640]{2,1,0:T(8,128)(2,1)S(1)}) custom-call(f32[1,16,1280]{2,1,0:T(8,128)} %latent.1, bf16[2,16,640]{2,1,0:T(8,128)(2,1)} %stale_k.1, bf16[2,16,640]{2,1,0:T(8,128)(2,1)} %stale_v.1, bf16[1,77,640]{2,1,0:T(8,128)(2,1)} %text_k.1, ...), custom_call_target="tpu_custom_call" | custom-call | tf_op jit(solution)/shard_map/pallas_call | solution.py:386
  31.7 0.6 %copy.18 = f32[1,16,1280]{2,1,0:T(8,128)} copy(f32[1,16,1280]{2,1,0:T(8,128)S(1)} %get-tuple-element.3) | data formatting | bytes 163840
  32.3 0.6 %copy.19 = bf16[2,16,640]{2,1,0:T(8,128)(2,1)} copy(bf16[2,16,640]{2,1,0:T(8,128)(2,1)S(1)} %get-tuple-element.4) | data formatting | bytes 81920
  33.0 0.6 %copy.20 = bf16[2,16,640]{2,1,0:T(8,128)(2,1)} copy(bf16[2,16,640]{2,1,0:T(8,128)(2,1)S(1)} %get-tuple-element.5) | data formatting | bytes 81920
